TPU v7x, 512 devices: a whole 4x4x16 slice. The times are simulated.
512 devices in a mesh: grp: 16 (over x, y), dev: 32 (over z, core).
Axes of the slice: x: 4, y: 4, z: 16, core: 2. Of those that a mesh axis runs over, the one named last changes fastest.
Arguments:
- block_vectors: float32 [262144, 64], P(('grp', 'dev')), may hold values from -6 to 6
- hamiltonian: float32 [4096, 64, 2048], P(('grp', 'dev')), may hold values from -0.125 to 0.125
- pattern: int32 [4096, 32], P(('grp', 'dev')), may hold values from 0 to 4095, as said below
- owned_blocks: int32 [512], P(('grp', 'dev')), may hold values from 1 to 8, as said below
- spectrum: float32 [2], replicated, may hold values from 0.5 to 2
Outputs:
- basis: float32 [262144, 64], P(('grp', 'dev'))
- r_factor: float32 [64, 64], replicated
Inputs may be any that keep to these rules, and one draw needn't show every extreme that they name: pattern[b, 0] = b; every other entry is b + o clipped to the slots, for a distinct nonzero o with |o| <= 16. `owned_blocks`: some device owns all 8 slots.
All inputs are finite; a program needn't handle non-finite values.
Results may differ from a plain program's by a relative error of at most 0.0003.
Values sent between devices are 32-bit elements; how exact they have to be, the bound alone decides.
A program may use at most 64 MiB of HBM per device.

v0:
```python
import jax
import jax.numpy as jnp
from jax import lax
from jax.sharding import PartitionSpec as P

BAND = 16


def shifted(block, axis, distance):
    devices = range(lax.axis_size(axis))
    route = [(i - distance, i) for i in devices if i - distance in devices]
    return lax.ppermute(block, axis, route)


def send_direct(values, distance):
    return shifted(values, ("grp", "dev"), distance)


def extend_band(values, reach_dev):
    lowers = []
    uppers = []
    for distance in range(reach_dev, 0, -1):
        lowers.append(send_direct(values, distance))
    for distance in range(1, reach_dev + 1):
        uppers.append(send_direct(values, -distance))
    return jnp.concatenate(lowers + [values] + uppers, axis=0)


def apply_matrix(values, hamiltonian, local_index, reach_dev):
    extended = extend_band(values, reach_dev)
    block_count, neighbours = local_index.shape
    picked = jnp.take(extended, local_index, axis=0)
    picked = picked.reshape(block_count, neighbours * values.shape[1], values.shape[2])
    return jnp.einsum("gik,gkc->gic", hamiltonian, picked, precision=lax.Precision.HIGHEST)


def summed_gram(flat):
    local_gram = jnp.dot(
        flat.T, flat, precision=lax.Precision.HIGHEST, preferred_element_type=jnp.float32
    )
    return lax.psum(local_gram, ("grp", "dev"))


def cholesky_step(flat):
    gram_total = summed_gram(flat)
    upper = jnp.linalg.cholesky(gram_total).T
    ortho = jax.scipy.linalg.solve_triangular(upper.T, flat.T, lower=True).T
    return (ortho, upper)


def on_device(block_vectors, hamiltonian, pattern, owned_blocks, spectrum):
    block_count = pattern.shape[0]
    block_size = hamiltonian.shape[1]
    columns = block_vectors.shape[1]
    reach_dev = (BAND + block_count - 1) // block_count
    first_block = lax.axis_index(("grp", "dev")) * block_count
    local_index = pattern - first_block + reach_dev * block_count
    live_mask = (jnp.arange(block_count, dtype=jnp.int32) < owned_blocks[0]).astype(jnp.float32)[
        :, None, None
    ]
    shift_value = spectrum[0]
    scale_value = spectrum[1]
    first_vec = block_vectors.reshape(block_count, block_size, columns) * live_mask
    second_vec = live_mask * (
        (apply_matrix(first_vec, hamiltonian, local_index, reach_dev) - shift_value * first_vec)
        / scale_value
    )
    third_vec = live_mask * (
        2.0
        * (apply_matrix(second_vec, hamiltonian, local_index, reach_dev) - shift_value * second_vec)
        / scale_value
        - first_vec
    )
    flat = third_vec.reshape(block_count * block_size, columns)
    ortho_one, upper_one = cholesky_step(flat)
    ortho_two, upper_two = cholesky_step(ortho_one)
    upper_all = jnp.dot(
        upper_two, upper_one, precision=lax.Precision.HIGHEST, preferred_element_type=jnp.float32
    )
    total = jnp.sqrt(
        jnp.float32(block_count * block_size * lax.axis_size("grp") * lax.axis_size("dev"))
    )
    return (ortho_two * total, upper_all / total)


def solution(mesh):
    placed = (
        P(("grp", "dev"), None),
        P(("grp", "dev"), None, None),
        P(("grp", "dev"), None),
        P(("grp", "dev")),
        P(),
    )
    return jax.shard_map(
        on_device,
        mesh=mesh,
        in_specs=placed,
        out_specs=(P(("grp", "dev"), None), P()),
        check_vma=False,
    )
```

profile of v0, /device:TPU:1, one launch (start us, length us, event | category | flops | bytes accessed | tf_op | source)
XLA Modules:
  0.0 355.4 jit_solution(15956783039810358615)
XLA Ops:
  3.7 8.8 %collective-permute-start.2 = (f32[8,64,64]{1,2,0:T(8,128)S(1)}, f32[8,64,64]{1,2,0:T(8,128)S(1)}, u32[]{:S(2)}, u32[]{:S(2)}) collective-permute-start(f32[8,64,64]{1,2,0:T(8,128)S(1)} %copy_multiply_fusion), channel_id=1, source_target_pairs={{1,0},{2,1},{3,2},{4,3},{5,4},{6,5},{7,6},{8,7},{9,8},{10,9},{11,1... | collective-permute-start | bytes 393224 | tf_op jit(solution)/shard_map/ppermute | solution.py:12
  12.5 4.2 %collective-permute-start.1 = (f32[8,64,64]{1,2,0:T(8,128)S(1)}, f32[8,64,64]{1,2,0:T(8,128)S(1)}, u32[]{:S(2)}, u32[]{:S(2)}) collective-permute-start(f32[8,64,64]{1,2,0:T(8,128)S(1)} %copy_multiply_fusion), channel_id=1, source_target_pairs={{0,1},{1,2},{2,3},{3,4},{4,5},{5,6},{6,7},{7,8},{8,9},{9,10},{10,1... | collective-permute-start | bytes 393224 | tf_op jit(solution)/shard_map/ppermute | solution.py:12
  20.8 4.5 %collective-permute-done = f32[8,64,64]{1,2,0:T(8,128)S(1)} collective-permute-done((f32[8,64,64]{1,2,0:T(8,128)S(1)}, f32[8,64,64]{1,2,0:T(8,128)S(1)}, u32[]{:S(2)}, u32[]{:S(2)}) %collective-permute-start) | collective-permute-done | bytes 131104 | tf_op jit(solution)/shard_map/ppermute | solution.py:12
  25.6 4.4 %gather_fusion = f32[256,64,64]{1,2,0:T(8,128)} fusion(f32[40,64,64]{1,2,0:T(8,128)S(1)} %constant_dynamic-update-slice_fusion, s32[1024]{0:T(1024)S(1)} %pad_clamp_fusion), kind=kCustom, calls=%fused_computation.clone | custom fusion | bytes 8389632 | tf_op jit(solution)/shard_map/jit(_take)/gather | solution.py:32
  29.9 3.8 %broadcast_select_fusion.1 = f32[8,32,64,64]{2,3,1,0:T(8,128)S(1)} fusion(f32[8,32,64,64]{2,3,1,0:T(8,128)} %bitcast.73, pred[8,32]{1,0:T(8,128)(4,1)S(1)} %get-tuple-element.4), kind=kLoop, calls=%fused_computation.3 | loop fusion | flops 1048576 | bytes 8388864 | tf_op jit(solution)/shard_map/jit(_take)/select_n | solution.py:32
  33.8 8.0 %copy.15 = f32[8,32,64,64]{2,1,3,0:T(8,128)} copy(f32[8,32,64,64]{2,3,1,0:T(8,128)S(1)} %broadcast_select_fusion.1) | data formatting | bytes 8388608 | tf_op jit(solution)/shard_map/jit(_take)/select_n | solution.py:32
  41.8 7.8 %reshape.35 = f32[8,2048,64]{1,2,0:T(8,128)} reshape(f32[8,32,64,64]{2,1,3,0:T(8,128)} %copy.15) | data formatting | bytes 8388608 | tf_op jit(solution)/shard_map/reshape | solution.py:33
  49.6 8.7 %fusion.4 = f32[8,64,64]{1,2,0:T(8,128)S(1)} fusion(f32[8,2048,64]{1,2,0:T(8,128)} %reshape.35, f32[8,64,2048]{2,1,0:T(8,128)} %param.11, f32[]{:T(128)} %bitcast.4, f32[]{:T(128)} %bitcast.3, f32[8]{0:T(128)S(1)} %compare_convert_fusion, f32[8,64,64]{1,0,2:T(8,128)S(1)} %reshape.34), kind=kOutput, calls=%fused_computation.10 | convolution fusion | flops 805470208 | bytes 8650792 | tf_op jit(solution)/shard_map/gik,gkc->gic/dot_general | solution.py:34
  58.3 4.1 %collective-permute-start.4 = (f32[8,64,64]{1,2,0:T(8,128)S(1)}, f32[8,64,64]{1,2,0:T(8,128)S(1)}, u32[]{:S(2)}, u32[]{:S(2)}) collective-permute-start(f32[8,64,64]{1,2,0:T(8,128)S(1)} %fusion.4), channel_id=1, source_target_pairs={{0,2},{1,3},{2,4},{3,5},{4,6},{5,7},{6,8},{7,9},{8,10},{9,11},{10,... | collective-permute-start | bytes 393224 | tf_op jit(solution)/shard_map/ppermute | solution.py:12
  62.4 2.7 collective-permute-start.5
  68.5 2.8 collective-permute-done.5
  71.3 6.5 %collective-permute-done.6 = f32[8,64,64]{1,2,0:T(8,128)S(1)} collective-permute-done((f32[8,64,64]{1,2,0:T(8,128)S(1)}, f32[8,64,64]{1,2,0:T(8,128)S(1)}, u32[]{:S(2)}, u32[]{:S(2)}) %collective-permute-start.6) | collective-permute-done | bytes 131104 | tf_op jit(solution)/shard_map/ppermute | solution.py:12
  77.9 4.4 %gather_fusion.1 = f32[256,64,64]{1,2,0:T(8,128)} fusion(f32[40,64,64]{1,2,0:T(8,128)S(1)} %constant_dynamic-update-slice_fusion.5, s32[1024]{0:T(1024)S(1)} %pad_clamp_fusion), kind=kCustom, calls=%fused_computation.1.clone | custom fusion | bytes 8389632 | tf_op jit(solution)/shard_map/jit(_take)/gather | solution.py:32
  82.2 3.8 %broadcast_select_fusion = f32[8,32,64,64]{2,3,1,0:T(8,128)S(1)} fusion(f32[8,32,64,64]{2,3,1,0:T(8,128)} %bitcast.72, pred[8,32]{1,0:T(8,128)(4,1)S(1)} %get-tuple-element.4), kind=kLoop, calls=%fused_computation.2 | loop fusion | flops 1048576 | bytes 8388864 | tf_op jit(solution)/shard_map/jit(_take)/select_n | solution.py:32
  86.1 8.0 %copy.16 = f32[8,32,64,64]{2,1,3,0:T(8,128)} copy(f32[8,32,64,64]{2,3,1,0:T(8,128)S(1)} %broadcast_select_fusion) | data formatting | bytes 8388608 | tf_op jit(solution)/shard_map/jit(_take)/select_n | solution.py:32
  94.1 7.8 %reshape.36 = f32[8,2048,64]{1,2,0:T(8,128)} reshape(f32[8,32,64,64]{2,1,3,0:T(8,128)} %copy.16) | data formatting | bytes 8388608 | tf_op jit(solution)/shard_map/reshape | solution.py:33
  101.9 8.7 %fusion.7 = f32[8,64,64]{1,2,0:T(8,128)S(1)} fusion(f32[8,2048,64]{1,2,0:T(8,128)} %reshape.36, f32[8,64,2048]{2,1,0:T(8,128)} %param.11, f32[8,64,64]{1,2,0:T(8,128)S(1)} %fusion.4, f32[]{:T(128)} %bitcast.4, f32[]{:T(128)} %bitcast.3, f32[8]{0:T(128)S(1)} %compare_convert_fusion, f32[8,64,64]{1,0,2:T(8,128)S(1)} %reshape.34), kind=kOutput, calls=%fused_computation.13 | convolution fusion | flops 805535744 | bytes 8781864 | tf_op jit(solution)/shard_map/gik,gkc->gic/dot_general | solution.py:34
  111.1 116.5 %psum.14 = f32[64,64]{0,1:T(8,128)S(1)} all-reduce(f32[64,64]{0,1:T(8,128)S(1)} %convolution_bitcast_fusion.2), channel_id=1, replica_groups=mesh['grp'=16,'dev'=32] {'grp','dev'}, use_global_device_ids=true, to_apply=%region_0.0 | all-reduce | flops 4096 | bytes 32768 | tf_op jit(solution)/shard_map/psum | solution.py:41
  227.9 5.8 %cholesky.44 = f32[64,64]{1,0:T(8,128)S(1)} custom-call(f32[64,64]{1,0:T(8,128)S(1)} %fusion.14), custom_call_target="Cholesky" | custom-call | tf_op jit(solution)/shard_map/jit(cholesky)/cholesky | solution.py:46
  235.1 4.9 %custom-call.6 = f32[1,64,64]{1,2,0:T(8,128)S(1)} custom-call(f32[1,64,64]{2,1,0:T(8,128)S(1)} %fusion.18), custom_call_target="InvertDiagBlocksLowerTriangular" | custom-call | tf_op jit(solution)/shard_map/jit(_solve_triangular)/triangular_solve | solution.py:47
  240.6 99.3 %psum.15 = f32[64,64]{0,1:T(8,128)S(1)} all-reduce(f32[64,64]{0,1:T(8,128)S(1)} %fusion.30), channel_id=1, replica_groups=mesh['grp'=16,'dev'=32] {'grp','dev'}, use_global_device_ids=true, to_apply=%region_3.7 | all-reduce | flops 4096 | bytes 32768 | tf_op jit(solution)/shard_map/psum | solution.py:41
  340.0 5.8 %cholesky.55 = f32[64,64]{1,0:T(8,128)S(1)} custom-call(f32[64,64]{1,0:T(8,128)S(1)} %fusion.12), custom_call_target="Cholesky" | custom-call | tf_op jit(solution)/shard_map/jit(cholesky)/cholesky | solution.py:46
  346.6 2.2 convolution_multiply_fusion.1
  349.5 4.9 %custom-call.7 = f32[1,64,64]{1,2,0:T(8,128)S(1)} custom-call(f32[1,64,64]{2,1,0:T(8,128)S(1)} %select_bitcast_fusion), custom_call_target="InvertDiagBlocksLowerTriangular" | custom-call | tf_op jit(solution)/shard_map/jit(_solve_triangular)/triangular_solve | solution.py:47
  (42 shorter events, 15.4 us)
Async XLA Ops:
  2.4 23.1 %collective-permute-start.3 = (f32[8,64,64]{1,2,0:T(8,128)S(1)}, f32[8,64,64]{1,2,0:T(8,128)S(1)}, u32[]{:S(2)}, u32[]{:S(2)}) collective-permute-start(f32[8,64,64]{1,2,0:T(8,128)S(1)} %copy_multiply_fusion), channel_id=1, source_target_pairs={{2,0},{3,1},{4,2},{5,3},{6,4},{7,5},{8,6},{9,7},{10,8},{11,9},{12,... | collective-permute-start | bytes 393224 | tf_op jit(solution)/shard_map/ppermute | solution.py:12
  3.7 21.8 %collective-permute-start.2 = (f32[8,64,64]{1,2,0:T(8,128)S(1)}, f32[8,64,64]{1,2,0:T(8,128)S(1)}, u32[]{:S(2)}, u32[]{:S(2)}) collective-permute-start(f32[8,64,64]{1,2,0:T(8,128)S(1)} %copy_multiply_fusion), channel_id=1, source_target_pairs={{1,0},{2,1},{3,2},{4,3},{5,4},{6,5},{7,6},{8,7},{9,8},{10,9},{11,1... | collective-permute-start | bytes 393224 | tf_op jit(solution)/shard_map/ppermute | solution.py:12
  12.5 12.9 %collective-permute-start.1 = (f32[8,64,64]{1,2,0:T(8,128)S(1)}, f32[8,64,64]{1,2,0:T(8,128)S(1)}, u32[]{:S(2)}, u32[]{:S(2)}) collective-permute-start(f32[8,64,64]{1,2,0:T(8,128)S(1)} %copy_multiply_fusion), channel_id=1, source_target_pairs={{0,1},{1,2},{2,3},{3,4},{4,5},{5,6},{6,7},{7,8},{8,9},{9,10},{10,1... | collective-permute-start | bytes 393224 | tf_op jit(solution)/shard_map/ppermute | solution.py:12
  16.7 8.7 %collective-permute-start = (f32[8,64,64]{1,2,0:T(8,128)S(1)}, f32[8,64,64]{1,2,0:T(8,128)S(1)}, u32[]{:S(2)}, u32[]{:S(2)}) collective-permute-start(f32[8,64,64]{1,2,0:T(8,128)S(1)} %copy_multiply_fusion), channel_id=1, source_target_pairs={{0,2},{1,3},{2,4},{3,5},{4,6},{5,7},{6,8},{7,9},{8,10},{9,11},{10,... | collective-permute-start | bytes 393224 | tf_op jit(solution)/shard_map/ppermute | solution.py:12
  58.3 10.2 %collective-permute-start.4 = (f32[8,64,64]{1,2,0:T(8,128)S(1)}, f32[8,64,64]{1,2,0:T(8,128)S(1)}, u32[]{:S(2)}, u32[]{:S(2)}) collective-permute-start(f32[8,64,64]{1,2,0:T(8,128)S(1)} %fusion.4), channel_id=1, source_target_pairs={{0,2},{1,3},{2,4},{3,5},{4,6},{5,7},{6,8},{7,9},{8,10},{9,11},{10,... | collective-permute-start | bytes 393224 | tf_op jit(solution)/shard_map/ppermute | solution.py:12
  62.4 8.9 %collective-permute-start.5 = (f32[8,64,64]{1,2,0:T(8,128)S(1)}, f32[8,64,64]{1,2,0:T(8,128)S(1)}, u32[]{:S(2)}, u32[]{:S(2)}) collective-permute-start(f32[8,64,64]{1,2,0:T(8,128)S(1)} %fusion.4), channel_id=1, source_target_pairs={{0,1},{1,2},{2,3},{3,4},{4,5},{5,6},{6,7},{7,8},{8,9},{9,10},{10,1... | collective-permute-start | bytes 393224 | tf_op jit(solution)/shard_map/ppermute | solution.py:12
  65.1 12.8 %collective-permute-start.7 = (f32[8,64,64]{1,2,0:T(8,128)S(1)}, f32[8,64,64]{1,2,0:T(8,128)S(1)}, u32[]{:S(2)}, u32[]{:S(2)}) collective-permute-start(f32[8,64,64]{1,2,0:T(8,128)S(1)} %fusion.4), channel_id=1, source_target_pairs={{2,0},{3,1},{4,2},{5,3},{6,4},{7,5},{8,6},{9,7},{10,8},{11,9},{12,... | collective-permute-start | bytes 393224 | tf_op jit(solution)/shard_map/ppermute | solution.py:12
  66.4 11.4 %collective-permute-start.6 = (f32[8,64,64]{1,2,0:T(8,128)S(1)}, f32[8,64,64]{1,2,0:T(8,128)S(1)}, u32[]{:S(2)}, u32[]{:S(2)}) collective-permute-start(f32[8,64,64]{1,2,0:T(8,128)S(1)} %fusion.4), channel_id=1, source_target_pairs={{1,0},{2,1},{3,2},{4,3},{5,4},{6,5},{7,6},{8,7},{9,8},{10,9},{11,1... | collective-permute-start | bytes 393224 | tf_op jit(solution)/shard_map/ppermute | solution.py:12
where the time goes:
time: 356 us; the launch traced here: 355 us
  blocking collectives  216 us (61%)
  local copies, waits for them, and re-layouts  43.3 us (12%)
  other arithmetic  32.9 us (9%)
  starting transfers between devices  26.5 us (7%)
  matrix products  21.5 us (6%)
  waiting for transfers between devices  13.8 us (4%)
    psum x2, blocking collectives, summed_gram(): return lax.psum(local_gram, ('grp', 'dev'))  216 us
    ppermute x8, starting transfers between devices, shifted(): return lax.ppermute(block, axis, route)  26.5 us
    dot_general x2, matrix products, apply_matrix(): jnp.einsum('gik,gkc->gic', hamiltonian, picked, precision=lax.Precision.H...  17.4 us
    select_n x2, local copies, waits for them, and re-layouts, apply_matrix(): picked = jnp.take(extended, local_index, axis=0)  16 us
    reshape x2, local copies, waits for them, and re-layouts, apply_matrix(): picked.reshape(block_count, neighbours * values.shape[1], values.shape[2])  15.6 us
    ppermute x8, waiting for transfers between devices, shifted(): return lax.ppermute(block, axis, route)  13.8 us
    another operation x6, other arithmetic, cholesky_step(): upper = jnp.linalg.cholesky(gram_total).T  13.1 us
    another operation x4, other arithmetic, cholesky_step(): ortho = jax.scipy.linalg.solve_triangular(upper.T, flat.T, lower=True).T  11.1 us
  transfers between devices with their start and end apart: 8, of which 3 were waited for; matrix products, arithmetic and copies ran while one was open for 1% of the time, Pallas kernels for 0%

commit v1 on v0

--- a/solution.py
+++ b/solution.py
@@ -4,6 +4,12 @@
 from jax.sharding import PartitionSpec as P
 
 BAND = 16
+
+
+def add_all(shard, mesh_axis):
+    parts = lax.all_gather(shard, mesh_axis, axis=0, tiled=False)
+    total = parts.sum(axis=0)
+    return total
 
 
 def shifted(block, axis, distance):
@@ -38,7 +44,7 @@
     local_gram = jnp.dot(
         flat.T, flat, precision=lax.Precision.HIGHEST, preferred_element_type=jnp.float32
     )
-    return lax.psum(local_gram, ("grp", "dev"))
+    return add_all(local_gram, ("grp", "dev"))
 
 
 def cholesky_step(flat):

time: 356 us -> 611 us (1.72)
  waiting for transfers between devices: 13.8 us -> 456 us
  blocking collectives: 216 us -> 0 us
  other arithmetic: 32.9 us -> 46.7 us
  between operations: 1.58 us -> 15 us
    all_gather x0 -> x2, waiting for transfers between devices: none -> 442 us  [add_all(): parts = lax.all_gather(shard, mesh_axis, axis=0, tiled=False)]
    psum x2 -> x0, blocking collectives: 216 us -> none  [summed_gram(): return lax.psum(local_gram, ('grp', 'dev'))]
    reduce_sum x0 -> x2, other arithmetic: none -> 13.9 us  [add_all(): total = parts.sum(axis=0)]
  transfers between devices with their start and end apart: 8 -> 10, of which waited for: 3 -> 5; matrix products, arithmetic and copies ran while one was open for 1% -> 0% of each run, Pallas kernels for 0% -> 0%
where the time goes in v1:
time: 611 us
  waiting for transfers between devices  456 us (75%)
  other arithmetic  46.7 us (8%)
  local copies, waits for them, and re-layouts  43.3 us (7%)
  starting transfers between devices  26.8 us (4%)
  matrix products  22.7 us (4%)
  between operations  15 us (2%)
    all_gather x2, waiting for transfers between devices, add_all(): parts = lax.all_gather(shard, mesh_axis, axis=0, tiled=False)  442 us
    ppermute x8, starting transfers between devices, shifted(): return lax.ppermute(block, axis, route)  26.5 us
    dot_general x2, matrix products, apply_matrix(): jnp.einsum('gik,gkc->gic', hamiltonian, picked, precision=lax.Precision.H...  17.4 us
    select_n x2, local copies, waits for them, and re-layouts, apply_matrix(): picked = jnp.take(extended, local_index, axis=0)  16 us
    reshape x2, local copies, waits for them, and re-layouts, apply_matrix(): picked.reshape(block_count, neighbours * values.shape[1], values.shape[2])  15.6 us
    ppermute x8, waiting for transfers between devices, shifted(): return lax.ppermute(block, axis, route)  14 us
    reduce_sum x2, other arithmetic, add_all(): total = parts.sum(axis=0)  13.9 us
    another operation x6, other arithmetic, cholesky_step(): upper = jnp.linalg.cholesky(gram_total).T  13.1 us
  transfers between devices with their start and end apart: 10, of which 5 were waited for; matrix products, arithmetic and copies ran while one was open for 0% of the time, Pallas kernels for 0%

profile of v1, /device:TPU:1, one launch (start us, length us, event | category | flops | bytes accessed | tf_op | source)
XLA Modules:
  0.0 610.5 jit_solution(17217625274676176439)
XLA Ops:
  10.3 8.8 %collective-permute-start.2 = (f32[8,64,64]{1,2,0:T(8,128)S(1)}, f32[8,64,64]{1,2,0:T(8,128)S(1)}, u32[]{:S(2)}, u32[]{:S(2)}) collective-permute-start(f32[8,64,64]{1,2,0:T(8,128)S(1)} %copy_multiply_fusion), channel_id=1, source_target_pairs={{1,0},{2,1},{3,2},{4,3},{5,4},{6,5},{7,6},{8,7},{9,8},{10,9},{11,1... | collective-permute-start | bytes 393224 | tf_op jit(solution)/shard_map/ppermute | solution.py:18
  19.1 4.2 collective-permute-start.1
  27.4 4.5 collective-permute-done
  32.1 4.4 gather_fusion
  36.5 3.8 broadcast_select_fusion.1
  40.3 8.0 %copy.20 = f32[8,32,64,64]{2,1,3,0:T(8,128)} copy(f32[8,32,64,64]{2,3,1,0:T(8,128)S(1)} %broadcast_select_fusion.1) | data formatting | bytes 8388608 | tf_op jit(solution)/shard_map/jit(_take)/select_n | solution.py:38
  48.3 7.8 %reshape.35 = f32[8,2048,64]{1,2,0:T(8,128)} reshape(f32[8,32,64,64]{2,1,3,0:T(8,128)} %copy.20) | data formatting | bytes 8388608 | tf_op jit(solution)/shard_map/reshape | solution.py:39
  56.2 8.7 %fusion.4 = f32[8,64,64]{1,2,0:T(8,128)S(1)} fusion(f32[8,2048,64]{1,2,0:T(8,128)} %reshape.35, f32[8,64,2048]{2,1,0:T(8,128)} %param.11, f32[]{:T(128)} %bitcast.4, f32[]{:T(128)} %bitcast.3, f32[8]{0:T(128)S(1)} %compare_convert_fusion, f32[8,64,64]{1,0,2:T(8,128)S(1)} %reshape.34), kind=kOutput, calls=%fused_computation.10 | convolution fusion | flops 805470208 | bytes 8650792 | tf_op jit(solution)/shard_map/gik,gkc->gic/dot_general | solution.py:40
  64.8 4.1 collective-permute-start.4
  75.1 2.8 collective-permute-done.5
  77.9 6.7 %collective-permute-done.6 = f32[8,64,64]{1,2,0:T(8,128)S(1)} collective-permute-done((f32[8,64,64]{1,2,0:T(8,128)S(1)}, f32[8,64,64]{1,2,0:T(8,128)S(1)}, u32[]{:S(2)}, u32[]{:S(2)}) %collective-permute-start.6) | collective-permute-done | bytes 131104 | tf_op jit(solution)/shard_map/ppermute | solution.py:18
  84.6 4.4 gather_fusion.1
  89.0 3.8 broadcast_select_fusion
  92.8 8.0 %copy.21 = f32[8,32,64,64]{2,1,3,0:T(8,128)} copy(f32[8,32,64,64]{2,3,1,0:T(8,128)S(1)} %broadcast_select_fusion) | data formatting | bytes 8388608 | tf_op jit(solution)/shard_map/jit(_take)/select_n | solution.py:38
  100.8 7.8 %reshape.36 = f32[8,2048,64]{1,2,0:T(8,128)} reshape(f32[8,32,64,64]{2,1,3,0:T(8,128)} %copy.21) | data formatting | bytes 8388608 | tf_op jit(solution)/shard_map/reshape | solution.py:39
  108.7 8.7 %fusion.7 = f32[8,64,64]{1,2,0:T(8,128)S(1)} fusion(f32[8,2048,64]{1,2,0:T(8,128)} %reshape.36, f32[8,64,2048]{2,1,0:T(8,128)} %param.11, f32[8,64,64]{1,2,0:T(8,128)S(1)} %fusion.4, f32[]{:T(128)} %bitcast.4, f32[]{:T(128)} %bitcast.3, f32[8]{0:T(128)S(1)} %compare_convert_fusion, f32[8,64,64]{1,0,2:T(8,128)S(1)} %reshape.34), kind=kOutput, calls=%fused_computation.13 | convolution fusion | flops 805535744 | bytes 8781864 | tf_op jit(solution)/shard_map/gik,gkc->gic/dot_general | solution.py:40
  118.9 226.5 %all-gather.5.cloned.1.call-done = f32[32768,64]{1,0:T(8,128)} async-done(((f32[64,64]{1,0:T(8,128)}), f32[32768,64]{1,0:T(8,128)}) %all-gather.5.cloned.1.call-update) | async-done | bytes 8388624 | tf_op jit(solution)/shard_map/all_gather | solution.py:10
  345.4 6.9 %reduce_sum.18 = f32[64,64]{1,0:T(8,128)S(1)} reduce(f32[512,64,64]{2,1,0:T(8,128)} %bitcast.76, f32[]{:T(128)} %constant.62.clone.1), dimensions={0}, to_apply=%region_0.0 | reduce | flops 2093056 | bytes 8404996 | tf_op jit(solution)/shard_map/reduce_sum | solution.py:11
  352.4 5.8 cholesky.44
  359.6 4.9 custom-call.6
  365.7 215.5 %all-gather.7.cloned.1.call-done = f32[32768,64]{1,0:T(8,128)} async-done(((f32[64,64]{1,0:T(8,128)}), f32[32768,64]{1,0:T(8,128)}) %all-gather.7.cloned.1.call-update) | async-done | bytes 8388624 | tf_op jit(solution)/shard_map/all_gather | solution.py:10
  581.2 6.9 %reduce_sum.19 = f32[64,64]{1,0:T(8,128)S(1)} reduce(f32[512,64,64]{2,1,0:T(8,128)} %bitcast.77, f32[]{:T(128)} %constant.62.clone.1), dimensions={0}, to_apply=%region_3.7 | reduce | flops 2093056 | bytes 8404996 | tf_op jit(solution)/shard_map/reduce_sum | solution.py:11
  588.3 5.8 cholesky.55
  597.8 4.9 custom-call.7
  (48 shorter events, 21.8 us)
Async XLA Ops:
  7.2 338.2 %all-gather.5.cloned.1.call-start = ((), (), s32[]{:S(2)}) async-start(), calls=%async_computation | async-start | bytes 16809984 | tf_op jit(solution)/shard_map/all_gather | solution.py:10
  9.0 23.1 %collective-permute-start.3 = (f32[8,64,64]{1,2,0:T(8,128)S(1)}, f32[8,64,64]{1,2,0:T(8,128)S(1)}, u32[]{:S(2)}, u32[]{:S(2)}) collective-permute-start(f32[8,64,64]{1,2,0:T(8,128)S(1)} %copy_multiply_fusion), channel_id=1, source_target_pairs={{2,0},{3,1},{4,2},{5,3},{6,4},{7,5},{8,6},{9,7},{10,8},{11,9},{12,... | collective-permute-start | bytes 393224 | tf_op jit(solution)/shard_map/ppermute | solution.py:18
  10.3 21.8 %collective-permute-start.2 = (f32[8,64,64]{1,2,0:T(8,128)S(1)}, f32[8,64,64]{1,2,0:T(8,128)S(1)}, u32[]{:S(2)}, u32[]{:S(2)}) collective-permute-start(f32[8,64,64]{1,2,0:T(8,128)S(1)} %copy_multiply_fusion), channel_id=1, source_target_pairs={{1,0},{2,1},{3,2},{4,3},{5,4},{6,5},{7,6},{8,7},{9,8},{10,9},{11,1... | collective-permute-start | bytes 393224 | tf_op jit(solution)/shard_map/ppermute | solution.py:18
  19.1 12.9 %collective-permute-start.1 = (f32[8,64,64]{1,2,0:T(8,128)S(1)}, f32[8,64,64]{1,2,0:T(8,128)S(1)}, u32[]{:S(2)}, u32[]{:S(2)}) collective-permute-start(f32[8,64,64]{1,2,0:T(8,128)S(1)} %copy_multiply_fusion), channel_id=1, source_target_pairs={{0,1},{1,2},{2,3},{3,4},{4,5},{5,6},{6,7},{7,8},{8,9},{9,10},{10,1... | collective-permute-start | bytes 393224 | tf_op jit(solution)/shard_map/ppermute | solution.py:18
  23.2 8.7 %collective-permute-start = (f32[8,64,64]{1,2,0:T(8,128)S(1)}, f32[8,64,64]{1,2,0:T(8,128)S(1)}, u32[]{:S(2)}, u32[]{:S(2)}) collective-permute-start(f32[8,64,64]{1,2,0:T(8,128)S(1)} %copy_multiply_fusion), channel_id=1, source_target_pairs={{0,2},{1,3},{2,4},{3,5},{4,6},{5,7},{6,8},{7,9},{8,10},{9,11},{10,... | collective-permute-start | bytes 393224 | tf_op jit(solution)/shard_map/ppermute | solution.py:18
  64.8 10.2 %collective-permute-start.4 = (f32[8,64,64]{1,2,0:T(8,128)S(1)}, f32[8,64,64]{1,2,0:T(8,128)S(1)}, u32[]{:S(2)}, u32[]{:S(2)}) collective-permute-start(f32[8,64,64]{1,2,0:T(8,128)S(1)} %fusion.4), channel_id=1, source_target_pairs={{0,2},{1,3},{2,4},{3,5},{4,6},{5,7},{6,8},{7,9},{8,10},{9,11},{10,... | collective-permute-start | bytes 393224 | tf_op jit(solution)/shard_map/ppermute | solution.py:18
  69.0 8.9 %collective-permute-start.5 = (f32[8,64,64]{1,2,0:T(8,128)S(1)}, f32[8,64,64]{1,2,0:T(8,128)S(1)}, u32[]{:S(2)}, u32[]{:S(2)}) collective-permute-start(f32[8,64,64]{1,2,0:T(8,128)S(1)} %fusion.4), channel_id=1, source_target_pairs={{0,1},{1,2},{2,3},{3,4},{4,5},{5,6},{6,7},{7,8},{8,9},{9,10},{10,1... | collective-permute-start | bytes 393224 | tf_op jit(solution)/shard_map/ppermute | solution.py:18
  71.7 12.9 %collective-permute-start.7 = (f32[8,64,64]{1,2,0:T(8,128)S(1)}, f32[8,64,64]{1,2,0:T(8,128)S(1)}, u32[]{:S(2)}, u32[]{:S(2)}) collective-permute-start(f32[8,64,64]{1,2,0:T(8,128)S(1)} %fusion.4), channel_id=1, source_target_pairs={{2,0},{3,1},{4,2},{5,3},{6,4},{7,5},{8,6},{9,7},{10,8},{11,9},{12,... | collective-permute-start | bytes 393224 | tf_op jit(solution)/shard_map/ppermute | solution.py:18
  73.1 11.4 %collective-permute-start.6 = (f32[8,64,64]{1,2,0:T(8,128)S(1)}, f32[8,64,64]{1,2,0:T(8,128)S(1)}, u32[]{:S(2)}, u32[]{:S(2)}) collective-permute-start(f32[8,64,64]{1,2,0:T(8,128)S(1)} %fusion.4), channel_id=1, source_target_pairs={{1,0},{2,1},{3,2},{4,3},{5,4},{6,5},{7,6},{8,7},{9,8},{10,9},{11,1... | collective-permute-start | bytes 393224 | tf_op jit(solution)/shard_map/ppermute | solution.py:18
  118.3 462.9 %all-gather.7.cloned.1.call-start = ((), (), s32[]{:S(2)}) async-start(), calls=%async_computation.1 | async-start | bytes 16809984 | tf_op jit(solution)/shard_map/all_gather | solution.py:10
Sparse Core Ops, SparseCore 0:
  118.5 226.8 all-gather.4
  365.8 215.3 all-gather.6
